TPU v7x, 32 devices: a whole 2x2x4 slice. The times are simulated.
32 devices in a mesh: parts: 2 (over x), req: 16 (over z, y, core).
Axes of the slice: x: 2, y: 2, z: 4, core: 2. Of those that a mesh axis runs over, the one named last changes fastest.
Arguments:
- conv_input: bfloat16 [32, 128, 8192], P(('parts', 'req')), parts along dimension 0, may hold values from -6 to 6
- gate_input: bfloat16 [32, 128, 8192], P(('parts', 'req')), parts along dimension 0, may hold values from -6 to 6
- step_size: bfloat16 [32, 128, 8192], P(('parts', 'req')), parts along dimension 0, may hold values from 7e-05 to 0.25
- state_maps: bfloat16 [32, 32, 128], P(('parts', 'req')), parts along dimension 0, may hold values from -12 to 12
- a_log: float32 [16, 8192], replicated, may hold values from 0 to 0.693
- conv_weight: bfloat16 [4, 8192], replicated, may hold values from -3 to 3
- conv_bias: float32 [8192], replicated, may hold values from -3 to 3
- skip_gain: float32 [8192], replicated, may hold values from 0.5 to 1.5
- owner_slot: int32 [32], P('parts'), parts along dimension 0, may hold values from 0 to 15, each once
- parent: int32 [32], P('parts'), parts along dimension 0, may hold values from 0 to 4, as said below
- lengths: int32 [32], P('parts'), parts along dimension 0, may hold values from 4 to 128, as said below
Outputs:
- scanned: bfloat16 [32, 128, 8192], P(('parts', 'req')), parts along dimension 0
There are 2 independent parts, one for each index of `parts`. A program takes and returns all parts, laid end to end along the dimension named above; an argument that names none is the same for every part. Nothing has to cross between parts.
Inputs may be any that keep to these rules, and one draw needn't show every extreme that they name: owner_slot[n] is the index along req of the device that holds node n; each index appears once. parent[0] is 0 and means no parent; nodes 1 to 4 have parent 0; every other node has a parent among nodes 1 to 4. lengths[n] live tokens stand at the start of node n's positions, the rest are padding; some node fills all 128.
All inputs are finite; a program needn't handle non-finite values.
Results may differ from a plain program's by a relative error of at most 0.001.
Values sent between devices are 32-bit elements; how exact they have to be, the bound alone decides.
A program may use at most 128 MiB of HBM per device.

v0:
```python
import jax
import jax.numpy as jnp
from jax import lax
from jax.sharding import PartitionSpec as P

FEW = 4


block_len = 8


def broadcast(block, axis, holder):
    block = jnp.where(lax.axis_index(axis) == holder, block, jnp.zeros_like(block))
    return lax.psum(block, axis)


def conv_rows(history, rows_x, conv_weight, conv_bias, row_count):
    extended = jnp.concatenate([history, rows_x], 0)
    pre_act = conv_bias[None, :]
    for k in range(conv_weight.shape[0]):
        pre_act = (
            pre_act + conv_weight[k].astype(jnp.float32)[None, :] * extended[k : k + row_count]
        )
    return jax.nn.silu(pre_act)


def scan_blocks(start_state, step_rows, input_rows, b_rows, c_rows, a_mat):
    slot_count, inner_width = step_rows.shape
    block_count = slot_count // block_len

    def advance(carry_state, pieces):
        step_block, input_block, b_block, c_block = pieces
        cum_steps = jnp.cumsum(step_block, 0)
        growth = jnp.exp(a_mat[None] * cum_steps[:, None, :])
        shrink = jnp.exp(-a_mat[None] * cum_steps[:, None, :])
        term_rows = shrink * b_block[:, :, None] * input_block[:, None, :]
        state_rows = growth * (carry_state[None] + jnp.cumsum(term_rows, 0))
        return (state_rows[-1], jnp.sum(c_block[:, :, None] * state_rows, 1))

    stacked = (
        step_rows.reshape(block_count, block_len, inner_width),
        input_rows.reshape(block_count, block_len, inner_width),
        b_rows.reshape(block_count, block_len, -1),
        c_rows.reshape(block_count, block_len, -1),
    )
    final_state, y_blocks = lax.scan(advance, start_state, stacked)
    return (final_state, y_blocks.reshape(slot_count, inner_width))


def body(
    conv_input,
    gate_input,
    step_size,
    state_maps,
    a_log,
    conv_weight,
    conv_bias,
    skip_gain,
    owner_slot,
    parent,
    lengths,
):
    x_rows = conv_input[0].astype(jnp.float32)
    delta_rows = step_size[0].astype(jnp.float32)
    states = a_log.shape[0]
    b_rows = state_maps[0][:states].astype(jnp.float32).T
    c_rows = state_maps[0][states:].astype(jnp.float32).T
    slot_count, inner_width = x_rows.shape
    rim_rows = conv_weight.shape[0] - 1
    a_mat = -jnp.exp(a_log)
    my_index = lax.axis_index("req")
    node_ids = jnp.arange(owner_slot.shape[0], dtype=jnp.int32)
    my_node = jnp.sum(jnp.where(owner_slot == my_index, node_ids, 0))
    is_mine = node_ids == my_node
    my_len = jnp.sum(jnp.where(is_mine, lengths, 0))
    my_parent = jnp.sum(jnp.where(is_mine, parent, 0))
    positions = jnp.arange(slot_count, dtype=jnp.int32)
    live_mask = (positions < my_len).astype(jnp.float32)[:, None]
    gate_act = jax.nn.silu(gate_input[0].astype(jnp.float32))
    zero_state = jnp.zeros((states, inner_width), jnp.float32)
    zero_history = jnp.zeros((rim_rows, inner_width), jnp.float32)

    def finish(y_rows, u_rows):
        return ((y_rows + skip_gain[None, :] * u_rows) * gate_act * live_mask).astype(jnp.bfloat16)

    def whole(start_state, history):
        extended = jnp.concatenate([history, x_rows], 0)
        u_rows = conv_rows(history, x_rows, conv_weight, conv_bias, slot_count)
        step_rows = delta_rows * live_mask
        final_state, y_rows = scan_blocks(
            start_state, step_rows, step_rows * u_rows, b_rows, c_rows, a_mat
        )
        tail_rows = lax.dynamic_slice_in_dim(extended, my_len, rim_rows, 0)
        return (finish(y_rows, u_rows), jnp.concatenate([final_state, tail_rows], 0))

    blank_pair = (
        jnp.zeros((slot_count, inner_width), jnp.bfloat16),
        jnp.zeros((states + rim_rows, inner_width), jnp.float32),
    )
    my_level = jnp.where(my_node == 0, 0, jnp.where(my_node <= FEW, 1, 2))
    first_pass = lax.cond(
        my_level == 0, lambda: whole(zero_state, zero_history), lambda: blank_pair
    )
    root_message = broadcast(first_pass[1], "req", owner_slot[0])
    second = lax.cond(
        my_level == 1,
        lambda: whole(root_message[:states], root_message[states:]),
        lambda: blank_pair,
    )
    few_ids = jnp.arange(FEW, dtype=jnp.int32) + 1
    pick_slot = (few_ids == my_node).astype(jnp.float32)
    few_messages = lax.psum(pick_slot[:, None, None] * second[1][None], "req")
    choose = (few_ids == my_parent).astype(jnp.float32)
    parent_message = jnp.sum(choose[:, None, None] * few_messages, 0)
    third_pass = lax.cond(
        my_level == 2,
        lambda: whole(parent_message[:states], parent_message[states:]),
        lambda: blank_pair,
    )
    result = jnp.where(
        my_level == 0, first_pass[0], jnp.where(my_level == 1, second[0], third_pass[0])
    )
    return result[None]


def solution(mesh):
    return jax.shard_map(
        body,
        mesh=mesh,
        in_specs=(
            P(("parts", "req"), None, None),
            P(("parts", "req"), None, None),
            P(("parts", "req"), None, None),
            P(("parts", "req"), None, None),
            P(),
            P(),
            P(),
            P(),
            P("parts"),
            P("parts"),
            P("parts"),
        ),
        out_specs=P(("parts", "req"), None, None),
        check_vma=False,
    )
```

profile of v0, /device:TPU:0, one launch (start us, length us, event | category | flops | bytes accessed | tf_op | source)
XLA Modules:
  0.0 501.1 jit_solution(10780403899443066101)
XLA Ops:
  9.9 1.9 fusion.61
  14.7 4.7 convert_multiply_fusion
  19.4 4.2 bitcast_convert_fusion
  23.6 1.6 conditional.3
  23.7 1.5 broadcast_in_dim.20
  26.9 181.2 %all-reduce.4.cloned.1.call-done = f32[19,8192]{1,0:T(8,128)} async-done(((f32[19,8192]{1,0:T(8,128)}), f32[19,8192]{1,0:T(8,128)}) %all-reduce.4.cloned.1.call-update) | async-done | bytes 622608 | tf_op jit(solution)/shard_map/psum | solution.py:14
  208.1 1.6 conditional.4
  208.2 1.5 broadcast_in_dim.41
  209.7 2.0 broadcast_multiply_fusion
  213.7 190.5 %all-reduce.6.cloned.1.call-done = f32[4,19,8192]{2,1,0:T(8,128)} async-done(((f32[4,19,8192]{2,1,0:T(8,128)}), f32[4,19,8192]{2,1,0:T(8,128)}) %all-reduce.6.cloned.1.call-update) | async-done | bytes 2490384 | tf_op jit(solution)/shard_map/psum | solution.py:112
  404.2 88.5 %conditional.5 = (bf16[128,8192]{1,0:T(8,128)(2,1)S(1)}) conditional(s32[]{:T(128)} %convert_element_type.106, () %tuple.55, (f32[4,1,1]{0,2,1:T(1,128)S(1)}, f32[4,19,8192]{2,1,0:T(8,128)}, f32[128,1]{0,1:T(1,128)S(1)}, f32[128,8192]{1,0:T(8,128)}, f32[8192]{0:T(1024)S(1)}, /*index=5*/bf16[4,8192]{1,0:T(4,128)(2,1)S(1)}, f32[128,8192]{1,0:T(8,128)}, ...), branch_computations={%region_19.20_spmd, %region_20.27_spmd} | conditional | flops 40443904 | bytes 68030744 | solution.py:115
  404.2 2.5 multiply_reduce_fusion.3
  407.3 8.3 %multiply_bitcast_fusion.4 = (f32[16,8,8192]{2,1,0:T(8,128)}, f32[128,8192]{1,0:T(8,128)}, f32[16,8,8192]{2,1,0:T(8,128)}) fusion(f32[128,8192]{1,0:T(8,128)} %get-tuple-element.347, f32[128]{0:T(128)S(1)} %bitcast.181, f32[128,8192]{1,0:T(8,128)S(1)} %copy-done.2, f32[8192]{0:T(1024)S(1)} %bitcast.170, f32[3,8192]{1,0:T(4,128)S(1)} %slice.111, ...), kind=kLoop, calls=%fused_computation.115 | loop fusion | flops 17825792 | bytes 21234176 | tf_op jit(solution)/shard_map/cond/branch_1_fun/reshape | solution.py:42
  415.6 71.4 %while.38 = (s32[]{:T(128)}, f32[16,8192]{1,0:T(8,128)S(1)}, f32[16,8,8192]{2,1,0:T(8,128)}, f32[16,8192]{1,0:T(8,128)S(1)}, f32[16,8,8192]{2,1,0:T(8,128)}, /*i...) while((s32[]{:T(128)}, f32[16,8192]{1,0:T(8,128)S(1)}, ...), condition=%wide.region_26.26_spmd, body=%wide.region_22.25_spmd.sunk | while | flops 16121858 | bytes 9702533 | solution.py:46
  416.9 2.4 multiply_reduce_fusion.7
  421.3 2.4 multiply_reduce_fusion.7
  425.8 2.4 multiply_reduce_fusion.7
  430.2 2.4 multiply_reduce_fusion.7
  434.7 2.4 multiply_reduce_fusion.7
  439.2 2.4 multiply_reduce_fusion.7
  443.6 2.4 multiply_reduce_fusion.7
  448.1 2.4 multiply_reduce_fusion.7
  452.6 2.4 multiply_reduce_fusion.7
  457.0 2.4 multiply_reduce_fusion.7
  461.5 2.4 multiply_reduce_fusion.7
  466.0 2.4 multiply_reduce_fusion.7
  470.4 2.4 multiply_reduce_fusion.7
  474.9 2.4 multiply_reduce_fusion.7
  479.3 2.4 multiply_reduce_fusion.7
  483.8 2.4 multiply_reduce_fusion.7
  486.9 5.7 %fusion.57 = bf16[128,8192]{1,0:T(8,128)(2,1)S(1)} fusion(f32[128,8192]{1,0:T(8,128)} %get-tuple-element.356, f32[16,8,8192]{2,1,0:T(8,128)} %get-tuple-element.354, f32[128,8192]{1,0:T(8,128)} %get-tuple-element.424, f32[8192]{0:T(1024)S(1)} %get-tuple-element.355, f32[128]{0:T(128)S(1)} %bitcast.182), kind=kLoop, calls=%fused_computation.114 | loop fusion | flops 5242880 | bytes 14713344 | tf_op jit(solution)/shard_map/cond/branch_1_fun/convert_element_type | solution.py:84
  492.6 1.6 select_bitcast_fusion
  (116 shorter events, 41.7 us)
Async XLA Ops:
  6.5 12.8 %copy-start.4 = (bf16[1,128,8192]{2,1,0:T(8,128)(2,1)S(1)}, bf16[1,128,8192]{2,1,0:T(8,128)(2,1)}, u32[]{:S(2)}) copy-start(bf16[1,128,8192]{2,1,0:T(8,128)(2,1)} %param.23) | copy-start | bytes 6291460
  6.5 201.6 %all-reduce.4.cloned.1.call-start = ((), (), s32[]{:S(2)}) async-start(), calls=%async_computation | async-start | bytes 1572864 | tf_op jit(solution)/shard_map/psum | solution.py:14
  13.4 6.0 %copy-start.5 = (bf16[1,128,8192]{2,1,0:T(8,128)(2,1)S(1)}, bf16[1,128,8192]{2,1,0:T(8,128)(2,1)}, u32[]{:S(2)}) copy-start(bf16[1,128,8192]{2,1,0:T(8,128)(2,1)} %param.25) | copy-start | bytes 6291460
  19.4 4.2 copy-start.3
  19.4 4.2 copy-start.6
  19.4 4.2 copy-start.7
  26.2 378.0 %all-reduce.6.cloned.1.call-start = ((), (), s32[]{:S(2)}) async-start(), calls=%async_computation.1 | async-start | bytes 6291456 | tf_op jit(solution)/shard_map/psum | solution.py:112
  209.7 2.0 copy-start.8
  404.2 3.1 copy-start.2
Sparse Core Ops, SparseCore 0:
  26.3 181.7 all-reduce.3
  212.1 191.9 all-reduce.5
where the time goes:
time: 502 us; the launch traced here: 501 us
  waiting for transfers between devices  372 us (74%)
  other arithmetic  79.4 us (16%)
  local copies, waits for them, and re-layouts  34 us (7%)
  between operations  15.4 us (3%)
    psum x1, waiting for transfers between devices, body(): few_messages = lax.psum(pick_slot[:, None, None] * second[1][None], 'req')  190 us
    psum x1, waiting for transfers between devices, broadcast(): return lax.psum(block, axis)  181 us
    another operation x16, other arithmetic, advance(): state_rows = growth * (carry_state[None] + jnp.cumsum(term_rows, 0))  38 us
    mul x16, local copies, waits for them, and re-layouts, advance(): term_rows = shrink * b_block[:, :, None] * input_block[:, None, :]  17 us
    dynamic_update_slice x16, local copies, waits for them, and re-layouts, scan_blocks(): final_state, y_blocks = lax.scan(advance, start_state, stacked)  11.7 us
  transfers between devices with their start and end apart: 2, of which 2 were waited for; matrix products, arithmetic and copies ran while one was open for 1% of the time, Pallas kernels for 0%

commit v1 on v0

v1 whole, which is shorter than its diff:
```python
import functools
import math

import jax
import jax.numpy as jnp
from jax import lax
from jax.experimental import pallas as pl
from jax.experimental.pallas import tpu as pltpu
from jax.sharding import PartitionSpec as P

FEW = 4
TILE = 1024
PAD = 8
STEPS = 8
LOG2E = math.log2(math.e)
VMEM_LIMIT = 40 * 1024 * 1024


def silu(v):
    half = 0.5 * v
    return half + half * jnp.tanh(half)


def prepare(rows, len_, first, x_ref, dt_ref, w_ref, bias_ref, xs, us, dts, xds):
    slots = x_ref.shape[1]
    t_ids = lax.broadcasted_iota(jnp.int32, (slots, 128), 0)
    live = jnp.logical_and(t_ids >= first, t_ids < len_).astype(jnp.float32)
    for c in range(8):
        cols = pl.ds(c * 128, 128)
        base = c * rows
        xs[pl.ds(base + PAD, slots), :] = x_ref[0, :, cols].astype(jnp.float32)
        pre = bias_ref[0:1, cols]
        for k in range(w_ref.shape[0]):
            pre = pre + w_ref[k : k + 1, cols].astype(jnp.float32) * xs[
                pl.ds(base + PAD - w_ref.shape[0] + 1 + k, slots), :
            ]
        u = silu(pre)
        dt = dt_ref[0, :, cols].astype(jnp.float32) * live
        if us is not None:
            us[pl.ds(base, slots), :] = u
        dts[pl.ds(base, slots), :] = dt
        xds[pl.ds(base, slots), :] = dt * u


def tile_of(ref, rows, t):
    return ref[pl.ds(t, 8, stride=rows), :]


def state_kernel(
    groups, len_ref, maps_ref, x_ref, dt_ref, btile_ref, a_ref, w_ref, bias_ref, msg_ref, xs, dts, xds
):
    slots = x_ref.shape[1]
    rows = slots + PAD
    states = a_ref.shape[1]
    span = states // groups
    rim = w_ref.shape[0] - 1
    length = len_ref[0]
    prepare(rows, length, rim, x_ref, dt_ref, w_ref, bias_ref, xs, None, dts, xds)
    a = [a_ref[0, j] for j in range(states)]

    def steps(i, carry):
        h, total = list(carry[:-1]), carry[-1]
        for k in range(STEPS):
            t = i * STEPS + k
            dt = tile_of(dts, rows, t)
            xd = tile_of(xds, rows, t)
            for j in range(states):
                h[j] = jnp.exp2(a[j] * dt) * h[j] + maps_ref[t * 2 * states + j] * xd
            total = total + dt
        return (*h, total)

    zero = jnp.zeros((8, 128), jnp.float32)
    out = lax.fori_loop(0, slots // STEPS, steps, (zero,) * (states + 1))
    for g in range(groups):
        for j in range(span):
            msg_ref[g, j] = out[g * span + j]
        msg_ref[g, span] = out[states]
        for r in range(rim):
            msg_ref[g, span + 1 + r] = tile_of(xs, rows, PAD + r)
            msg_ref[g, span + 1 + 2 * rim + r] = tile_of(xs, rows, PAD + length - rim + r)
        msg_ref[g, span + 1 + 3 * rim] = btile_ref[g]
    for c in range(8):
        dts[pl.ds(c * rows, 8), :] = dt_ref[0, 0:8, pl.ds(c * 128, 128)].astype(jnp.float32)
    for g in range(groups):
        for r in range(rim):
            msg_ref[g, span + 1 + rim + r] = tile_of(dts, rows, r)


def exchange_kernel(
    groups, owner_ref, sel_ref, msg_ref, a_ref, w_ref, bias_ref, out_ref,
    recv, table, back, send1, recv1, send2, recv2, local_sem,
):
    n = msg_ref.shape[0]
    span = a_ref.shape[1] // groups
    taps = w_ref.shape[0]
    rim = taps - 1
    me = lax.axis_index("req")
    tile = me // groups
    first = (me % groups) * span

    barrier = pltpu.get_barrier_semaphore()

    def greet(k, c):
        pl.semaphore_signal(
            barrier, inc=1, device_id={"req": (me + k) % n}, device_id_type=pl.DeviceIdType.MESH
        )
        return c

    lax.fori_loop(1, n, greet, 0)
    pl.semaphore_wait(barrier, n - 1)

    def out_copy(k):
        to = (me + k) % n
        return pltpu.make_async_remote_copy(
            src_ref=msg_ref.at[to], dst_ref=recv.at[me],
            send_sem=send1.at[k], recv_sem=recv1.at[me],
            device_id={"req": to}, device_id_type=pl.DeviceIdType.MESH,
        )

    def in_copy(k):
        source = (me + k) % n
        return pltpu.make_async_remote_copy(
            src_ref=msg_ref.at[me], dst_ref=recv.at[source],
            send_sem=send1.at[k], recv_sem=recv1.at[source],
            device_id={"req": source}, device_id_type=pl.DeviceIdType.MESH,
        )

    lax.fori_loop(1, n, lambda k, c: (out_copy(k).start(), c)[1], 0)
    own = pltpu.make_async_copy(msg_ref.at[me], recv.at[me], local_sem)
    own.start()
    own.wait()
    lax.fori_loop(1, n, lambda k, c: (in_copy(k).wait_recv(), c)[1], 0)

    a = [a_ref[tile, first + j] for j in range(span)]
    w = [w_ref[k, tile] for k in range(taps)]
    bias = bias_ref[tile]
    zero = jnp.zeros((8, 128), jnp.float32)

    def node(k, start, history):
        slot = owner_ref[k]
        rows = list(history) + [recv[slot, span + 1 + r] for r in range(rim)]
        btile = recv[slot, span + 1 + 3 * rim]
        h = list(start)
        for r in range(rim):
            pre = bias
            for q in range(taps):
                pre = pre + w[q] * rows[r + q]
            dt = recv[slot, span + 1 + rim + r]
            xd = dt * silu(pre)
            for j in range(span):
                h[j] = jnp.exp2(a[j] * dt) * h[j] + btile[j : j + 1, r : r + 1] * xd
        total = recv[slot, span]
        h = [jnp.exp2(a[j] * total) * h[j] + recv[slot, j] for j in range(span)]
        tail = [recv[slot, span + 1 + 2 * rim + r] for r in range(rim)]
        return h, tail

    for r in range(span + rim):
        table[0, r] = zero
    root_end, root_tail = node(0, [zero] * span, [zero] * rim)
    for r, value in enumerate(root_end + root_tail):
        table[1, r] = value
    for k in range(1, FEW + 1):
        end, tail = node(k, root_end, root_tail)
        for r, value in enumerate(end + tail):
            table[1 + k, r] = value

    def back_out(k):
        to = (me + k) % n
        return pltpu.make_async_remote_copy(
            src_ref=back.at[to], dst_ref=out_ref.at[me],
            send_sem=send2.at[k], recv_sem=recv2.at[me],
            device_id={"req": to}, device_id_type=pl.DeviceIdType.MESH,
        )

    def back_in(k):
        source = (me + k) % n
        return pltpu.make_async_remote_copy(
            src_ref=back.at[me], dst_ref=out_ref.at[source],
            send_sem=send2.at[k], recv_sem=recv2.at[source],
            device_id={"req": source}, device_id_type=pl.DeviceIdType.MESH,
        )

    def fill(to):
        back[to] = table[sel_ref[to]]

    def reply(k, c):
        fill((me + k) % n)
        back_out(k).start()
        return c

    lax.fori_loop(1, n, reply, 0)
    fill(me)
    own = pltpu.make_async_copy(back.at[me], out_ref.at[me], local_sem)
    own.start()
    own.wait()

    def finish(k, c):
        out_copy(k).wait_send()
        back_out(k).wait_send()
        back_in(k).wait_recv()
        return c

    lax.fori_loop(1, n, finish, 0)


def scan_kernel(
    groups, len_ref, maps_ref, x_ref, dt_ref, z_ref, start_ref, a_ref, w_ref, bias_ref, skip_ref,
    out_ref, xs, us, dts, xds, ys
):
    slots = x_ref.shape[1]
    rows = slots + PAD
    states = a_ref.shape[1]
    span = states // groups
    rim = w_ref.shape[0] - 1
    length = len_ref[0]
    for r in range(rim):
        xs[pl.ds(PAD - rim + r, 8, stride=rows), :] = start_ref[0, span + r]
    prepare(rows, length, 0, x_ref, dt_ref, w_ref, bias_ref, xs, us, dts, xds)
    a = [a_ref[0, j] for j in range(states)]

    def steps(i, carry):
        h = list(carry)
        for k in range(STEPS):
            t = i * STEPS + k
            dt = tile_of(dts, rows, t)
            xd = tile_of(xds, rows, t)
            parts = []
            for j in range(states):
                h[j] = jnp.exp2(a[j] * dt) * h[j] + maps_ref[t * 2 * states + j] * xd
                part = maps_ref[t * 2 * states + states + j] * h[j]
                if j < 2:
                    parts.append(part)
                else:
                    parts[j % 2] = parts[j % 2] + part
            ys[pl.ds(t, 8, stride=rows), :] = parts[0] + parts[1]
        return tuple(h)

    start = tuple(start_ref[j // span, j % span] for j in range(states))
    lax.fori_loop(0, slots // STEPS, steps, start)
    t_ids = lax.broadcasted_iota(jnp.int32, (slots, 128), 0)
    live = (t_ids < length).astype(jnp.float32)
    for c in range(8):
        cols = pl.ds(c * 128, 128)
        rows_c = pl.ds(c * rows, slots)
        y = ys[rows_c, :] + skip_ref[0:1, cols] * us[rows_c, :]
        gate = silu(z_ref[0, :, cols].astype(jnp.float32)) * live
        out_ref[0, :, cols] = (y * gate).astype(jnp.bfloat16)


def body(
    conv_input, gate_input, step_size, state_maps, a_log, conv_weight, conv_bias, skip_gain,
    owner_slot, parent, lengths,
):
    n = owner_slot.shape[0]
    _, slots, inner = conv_input.shape
    states = a_log.shape[0]
    taps = conv_weight.shape[0]
    rim = taps - 1
    tiles = inner // TILE
    groups = n // tiles
    span = states // groups
    rows = slots + PAD
    message = span + 2 + 3 * rim

    me = lax.axis_index("req")
    ids = jnp.arange(n, dtype=jnp.int32)
    holds = owner_slot[None, :] == ids[:, None]
    my_len = jnp.sum(jnp.where(owner_slot == me, lengths, 0)).reshape(1)
    source = jnp.where(ids == 0, 0, jnp.where(ids <= FEW, 1, parent + 1))
    sel = jnp.sum(jnp.where(holds, source[None, :], 0), 1)

    maps = state_maps[0].astype(jnp.float32)
    flat_maps = maps.T.reshape(-1)
    btile = jnp.pad(maps[:states].reshape(groups, span, slots), ((0, 0), (0, 8 - span), (0, 0)))
    btile = btile[:, :, :128]
    a2 = (-LOG2E * jnp.exp(a_log)).reshape(states, tiles, 8, 128).transpose(1, 0, 2, 3)
    w_tiles = conv_weight.astype(jnp.float32).reshape(taps, tiles, 8, 128)
    bias_tiles = conv_bias.reshape(tiles, 8, 128)
    bias_row = conv_bias[None]
    skip_row = skip_gain[None]

    smem = pl.BlockSpec(memory_space=pltpu.SMEM)
    vmem = pl.BlockSpec(memory_space=pltpu.VMEM)
    big = pl.BlockSpec((1, slots, TILE), lambda b: (0, 0, b))
    a_spec = pl.BlockSpec((1, states, 8, 128), lambda b: (b, 0, 0, 0))
    w_spec = pl.BlockSpec((taps, TILE), lambda b: (0, b))
    row_spec = pl.BlockSpec((1, TILE), lambda b: (0, b))
    columns = pltpu.VMEM((8 * rows, 128), jnp.float32)

    msg = pl.pallas_call(
        functools.partial(state_kernel, groups),
        grid=(tiles,),
        out_shape=jax.ShapeDtypeStruct((n, message, 8, 128), jnp.float32),
        in_specs=[
            smem, smem, big, big,
            pl.BlockSpec((groups, 8, 128), lambda b: (0, 0, 0)),
            a_spec, w_spec, row_spec,
        ],
        out_specs=pl.BlockSpec((groups, message, 8, 128), lambda b: (b, 0, 0, 0)),
        scratch_shapes=[columns] * 3,
        compiler_params=pltpu.CompilerParams(vmem_limit_bytes=VMEM_LIMIT),
        name="state_pass",
    )(my_len, flat_maps, conv_input, step_size, btile, a2, conv_weight, bias_row)

    starts = pl.pallas_call(
        functools.partial(exchange_kernel, groups),
        out_shape=jax.ShapeDtypeStruct((n, span + rim, 8, 128), jnp.float32),
        in_specs=[smem, smem, vmem, vmem, vmem, vmem],
        out_specs=vmem,
        scratch_shapes=[
            pltpu.VMEM((n, message, 8, 128), jnp.float32),
            pltpu.VMEM((FEW + 2, span + rim, 8, 128), jnp.float32),
            pltpu.VMEM((n, span + rim, 8, 128), jnp.float32),
            pltpu.SemaphoreType.DMA((n,)),
            pltpu.SemaphoreType.DMA((n,)),
            pltpu.SemaphoreType.DMA((n,)),
            pltpu.SemaphoreType.DMA((n,)),
            pltpu.SemaphoreType.DMA,
        ],
        compiler_params=pltpu.CompilerParams(
            vmem_limit_bytes=VMEM_LIMIT, collective_id=0, has_side_effects=True
        ),
        name="exchange",
    )(owner_slot, sel, msg, a2, w_tiles, bias_tiles)

    return pl.pallas_call(
        functools.partial(scan_kernel, groups),
        grid=(tiles,),
        out_shape=jax.ShapeDtypeStruct((1, slots, inner), jnp.bfloat16),
        in_specs=[
            smem, smem, big, big, big,
            pl.BlockSpec((groups, span + rim, 8, 128), lambda b: (b, 0, 0, 0)),
            a_spec, w_spec, row_spec, row_spec,
        ],
        out_specs=big,
        scratch_shapes=[columns] * 5,
        compiler_params=pltpu.CompilerParams(vmem_limit_bytes=VMEM_LIMIT),
        name="full_scan",
    )(my_len, flat_maps, conv_input, step_size, gate_input, starts, a2, conv_weight, bias_row, skip_row)


def solution(mesh):
    blocks = P(("parts", "req"), None, None)
    return jax.shard_map(
        body,
        mesh=mesh,
        in_specs=(
            blocks, blocks, blocks, blocks,
            P(), P(), P(), P(),
            P("parts"), P("parts"), P("parts"),
        ),
        out_specs=blocks,
        check_vma=False,
    )
```

time: 502 us -> 110 us (0.22)
  the two profiles are of different devices: /device:TPU:0 before, /device:TPU:21 now
where the time goes in v1:
time: 110 us
  Pallas kernels  102 us (93%)
  other arithmetic  5.6 us (5%)
  local copies, waits for them, and re-layouts  1.95 us (2%)
    pallas_call x1, Pallas kernels, body(): pl.pallas_call(functools.partial(exchange_kernel, groups), out_shape=jax....  54.4 us
    pallas_call x1, Pallas kernels, body(): pl.pallas_call(functools.partial(scan_kernel, groups), grid=(tiles,), out...  28.3 us
    pallas_call x1, Pallas kernels, body(): pl.pallas_call(functools.partial(state_kernel, groups), grid=(tiles,), ou...  19.4 us

profile of v1, /device:TPU:21, one launch (start us, length us, event | category | flops | bytes accessed | tf_op | source)
XLA Modules:
  0.0 109.8 jit_solution(12824971803826211845)
XLA Ops:
  0.0 0.0 copy-start.4
  0.0 0.0 copy-start.5
  0.0 0.0 copy-start
  0.0 1.5 %fusion = s32[]{:T(128)} fusion(s32[16]{0:T(128)} %param.21, s32[16]{0:T(128)} %owner_ref.1, s32[]{:T(128)S(6)} %axis_index.12), kind=kLoop, calls=%fused_computation.11 | loop fusion | flops 47 | bytes 136 | tf_op jit(solution)/shard_map/reduce_sum | solution.py:268
  1.5 0.7 compare_select_fusion.1
  2.2 0.8 select_reduce_fusion.sel_ref
  2.9 0.7 fusion.1
  3.6 0.1 copy.14
  3.7 0.1 reshape.26.maps_ref
  3.8 0.9 convert_bitcast_fusion
  4.7 1.1 %multiply_bitcast_fusion = f32[2,8,64,128]{3,1,2,0:T(8,128)S(1)} fusion(f32[16,8192]{1,0:T(8,128)} %param.15), kind=kLoop, calls=%fused_computation.1 | loop fusion | flops 131072 | bytes 1048576
  5.8 0.1 copy.16
  6.0 0.0 copy-done.4
  6.0 0.0 copy-done.5
  6.0 0.0 copy-done
  6.0 0.0 copy-start.1
  6.0 1.6 %copy-done.1 = bf16[1,128,8192]{2,1,0:T(8,128)(2,1)S(1)} copy-done((bf16[1,128,8192]{2,1,0:T(8,128)(2,1)S(1)}, bf16[1,128,8192]{2,1,0:T(8,128)(2,1)}, u32[]{:S(2)}) %copy-start.1) | copy-done | bytes 2097176
  7.6 0.0 copy-start.7
  7.6 0.0 copy-start.3
  7.6 19.4 %state_pass.1.msg_ref = f32[16,19,8,128]{3,2,1,0:T(8,128)S(1)} custom-call(s32[1]{0:T(128)} %bitcast.len_ref, f32[4096]{0:T(1024)S(1)} %reshape.26.maps_ref, bf16[1,128,8192]{2,1,0:T(8,128)(2,1)S(1)} %copy-done, bf16[1,128,8192]{2,1,0:T(8,128)(2,1)S(1)} %copy-done.1, f32[2,8,128]{2,1,0:T(8,128)S(1)} %slice_bitcast_fusion.btile_ref, ...), custom_call_target="tpu_custom_call" | custom-call | tf_op jit(solution)/shard_map/state_pass/pallas_call | solution.py:290
  27.0 0.0 copy-done.7
  27.0 0.0 copy-start.2
  27.0 0.0 copy-start.6
  27.1 54.4 %exchange.1.start_ref = f32[16,11,8,128]{3,2,1,0:T(8,128)S(1)} custom-call(s32[16]{0:T(128)S(1)} %copy-done.7, s32[16]{0:T(128)S(1)} %select_reduce_fusion.sel_ref, f32[16,19,8,128]{3,2,1,0:T(8,128)S(1)} %state_pass.1.msg_ref, f32[8,16,8,128]{3,2,1,0:T(8,128)S(1)} %bitcast.24, f32[4,8,8,128]{3,2,1,0:T(8,128)S(1)} %bitcast.26, f32[8,8,128]{2,1,0:T(8,128)S(1)} %bitcast.28), custom_call_target="tpu_custom_call" | custom-call | tf_op jit(solution)/shard_map/exchange/pallas_call | solution.py:305
  81.5 0.0 copy-done.3
  81.5 0.0 copy-done.2
  81.5 0.0 copy-done.6
  81.5 28.3 %full_scan.1 = bf16[1,128,8192]{2,1,0:T(8,128)(2,1)} custom-call(s32[1]{0:T(128)} %bitcast.len_ref, f32[4096]{0:T(1024)S(1)} %reshape.26.maps_ref, bf16[1,128,8192]{2,1,0:T(8,128)(2,1)S(1)} %copy-done, bf16[1,128,8192]{2,1,0:T(8,128)(2,1)S(1)} %copy-done.2, bf16[1,128,8192]{2,1,0:T(8,128)(2,1)S(1)} %copy-done.3, f32[16,11,8,128]{3,2,1,0:T(8,128)S(1)} %exchange.1.start_ref, ...), custom_call_target="tpu_custom_call" | custom-call | tf_op jit(solution)/shard_map/full_scan/pallas_call | solution.py:326
  (3 shorter events, 0.1 us)
Async XLA Ops:
  0.0 6.0 %copy-start.4 = (bf16[4,8192]{1,0:T(4,128)(2,1)S(1)}, bf16[4,8192]{1,0:T(4,128)(2,1)}, u32[]{:S(2)}) copy-start(bf16[4,8192]{1,0:T(4,128)(2,1)} %w_ref.3) | copy-start | bytes 196612
  0.0 6.0 %copy-start.5 = (f32[8192]{0:T(1024)S(1)}, f32[8192]{0:T(1024)}, u32[]{:S(2)}) copy-start(f32[8192]{0:T(1024)} %param.17) | copy-start | bytes 98308
  0.0 6.0 %copy-start = (bf16[1,128,8192]{2,1,0:T(8,128)(2,1)S(1)}, bf16[1,128,8192]{2,1,0:T(8,128)(2,1)}, u32[]{:S(2)}) copy-start(bf16[1,128,8192]{2,1,0:T(8,128)(2,1)} %x_ref.3) | copy-start | bytes 6291460
  6.0 1.6 %copy-start.1 = (bf16[1,128,8192]{2,1,0:T(8,128)(2,1)S(1)}, bf16[1,128,8192]{2,1,0:T(8,128)(2,1)}, u32[]{:S(2)}) copy-start(bf16[1,128,8192]{2,1,0:T(8,128)(2,1)} %dt_ref.3) | copy-start | bytes 6291460
  7.6 19.4 %copy-start.7 = (s32[16]{0:T(128)S(1)}, s32[16]{0:T(128)}, u32[]{:S(2)}) copy-start(s32[16]{0:T(128)} %owner_ref.1) | copy-start | bytes 196
  7.6 73.9 %copy-start.3 = (bf16[1,128,8192]{2,1,0:T(8,128)(2,1)S(1)}, bf16[1,128,8192]{2,1,0:T(8,128)(2,1)}, u32[]{:S(2)}) copy-start(bf16[1,128,8192]{2,1,0:T(8,128)(2,1)} %z_ref.1) | copy-start | bytes 6291460
  27.0 54.4 %copy-start.2 = (bf16[1,128,8192]{2,1,0:T(8,128)(2,1)S(1)}, bf16[1,128,8192]{2,1,0:T(8,128)(2,1)}, u32[]{:S(2)}) copy-start(bf16[1,128,8192]{2,1,0:T(8,128)(2,1)} %dt_ref.3) | copy-start | bytes 6291460
  27.0 54.4 %copy-start.6 = (f32[8192]{0:T(1024)S(1)}, f32[8192]{0:T(1024)}, u32[]{:S(2)}) copy-start(f32[8192]{0:T(1024)} %param.18) | copy-start | bytes 98308

commit v2 on v1

v2 whole, which is shorter than its diff:
```python
import functools
import math

import jax
import jax.numpy as jnp
from jax import lax
from jax.experimental import pallas as pl
from jax.experimental.pallas import tpu as pltpu
from jax.sharding import PartitionSpec as P

FEW = 4
TILE = 1024
PAD = 8
STEPS = 8
LOG2E = math.log2(math.e)
VMEM_LIMIT = 40 * 1024 * 1024


def silu(v):
    half = 0.5 * v
    return half + half * jnp.tanh(half)


def column(b, c):
    return pl.ds(pl.multiple_of(b * TILE + c * 128, 128), 128)


def prepare(rows, b, length, first, x_ref, dt_ref, w_ref, bias_ref, xs, us, dts, xds):
    slots = x_ref.shape[1]
    taps = w_ref.shape[0]
    t_ids = lax.broadcasted_iota(jnp.int32, (slots, 128), 0)
    live = jnp.logical_and(t_ids >= first, t_ids < length).astype(jnp.float32)
    for c in range(8):
        cols = column(b, c)
        base = c * rows
        xs[pl.ds(base + PAD, slots), :] = x_ref[0, :, cols].astype(jnp.float32)
        pre = bias_ref[0:1, cols]
        for k in range(taps):
            pre = pre + w_ref[k : k + 1, cols] * xs[pl.ds(base + PAD - taps + 1 + k, slots), :]
        u = silu(pre)
        dt = dt_ref[0, :, cols].astype(jnp.float32) * live
        if us is not None:
            us[pl.ds(base, slots), :] = u
        dts[pl.ds(base, slots), :] = dt
        xds[pl.ds(base, slots), :] = dt * u


def tile_of(ref, rows, t):
    return ref[pl.ds(t, 8, stride=rows), :]


def tree_kernel(
    groups, len_ref, maps_ref, owner_ref, sel_ref, x_ref, dt_ref, z_ref, btile_ref, a_ref,
    w_ref, bias_ref, skip_ref, w_tiles, bias_tiles, out_ref,
    xs, us, dts, xds, ys, msg, recv, table, back, starts, send1, recv1, send2, recv2, local_sem,
):
    n = msg.shape[0]
    slots = x_ref.shape[1]
    rows = slots + PAD
    tiles, states = a_ref.shape[:2]
    span = states // groups
    taps = w_ref.shape[0]
    rim = taps - 1
    me = lax.axis_index("req")
    tile = me // groups
    first = (me % groups) * span
    length = len_ref[0]
    zero = jnp.zeros((8, 128), jnp.float32)

    barrier = pltpu.get_barrier_semaphore()

    def greet(k, c):
        pl.semaphore_signal(
            barrier, inc=1, device_id={"req": (me + k) % n}, device_id_type=pl.DeviceIdType.MESH
        )
        return c

    lax.fori_loop(1, n, greet, 0)
    pl.semaphore_wait(barrier, n - 1)

    def copy(src, dst, slot, sends, recvs, device):
        return pltpu.make_async_remote_copy(
            src_ref=src, dst_ref=dst, send_sem=sends.at[device], recv_sem=recvs.at[slot],
            device_id={"req": device}, device_id_type=pl.DeviceIdType.MESH,
        )

    def up_out(to):
        return copy(msg.at[to], recv.at[me], me, send1, recv1, to)

    def up_in(source):
        return copy(msg.at[source], recv.at[source], source, send1, recv1, source)

    def down_out(to):
        return copy(back.at[to], starts.at[me], me, send2, recv2, to)

    def down_in(source):
        return copy(back.at[source], starts.at[source], source, send2, recv2, source)

    for c in range(8):
        xs[pl.ds(c * rows, PAD), :] = zero

    def state_pass(r, unused):
        b = (tile + r) % tiles
        prepare(rows, b, length, rim, x_ref, dt_ref, w_ref, bias_ref, xs, None, dts, xds)
        a = [a_ref[b, j] for j in range(states)]

        def steps(i, carry):
            h, total = list(carry[:-1]), carry[-1]
            for k in range(STEPS):
                t = i * STEPS + k
                dt = tile_of(dts, rows, t)
                xd = tile_of(xds, rows, t)
                for j in range(states):
                    h[j] = jnp.exp2(a[j] * dt) * h[j] + maps_ref[t * 2 * states + j] * xd
                total = total + dt
            return (*h, total)

        out = lax.fori_loop(0, slots // STEPS, steps, (zero,) * (states + 1))
        for c in range(8):
            dts[pl.ds(c * rows, 8), :] = dt_ref[0, 0:8, column(b, c)].astype(jnp.float32)
        for g in range(groups):
            to = b * groups + g
            for j in range(span):
                msg[to, j] = out[g * span + j]
            msg[to, span] = out[states]
            for q in range(rim):
                msg[to, span + 1 + q] = tile_of(xs, rows, PAD + q)
                msg[to, span + 1 + rim + q] = tile_of(dts, rows, q)
                msg[to, span + 1 + 2 * rim + q] = tile_of(xs, rows, PAD + length - rim + q)
            msg[to, span + 1 + 3 * rim] = btile_ref[g]

            @pl.when(to != me)
            def _():
                up_out(to).start()

        return unused

    lax.fori_loop(0, tiles, state_pass, 0)
    own = pltpu.make_async_copy(msg.at[me], recv.at[me], local_sem)
    own.start()
    own.wait()
    lax.fori_loop(1, n, lambda k, c: (up_in((me + k) % n).wait_recv(), c)[1], 0)

    a = [a_ref[tile, first + j] for j in range(span)]
    w = [w_tiles[k, tile] for k in range(taps)]
    bias = bias_tiles[tile]

    def node(k, start, history):
        slot = owner_ref[k]
        x = list(history) + [recv[slot, span + 1 + q] for q in range(rim)]
        btile = recv[slot, span + 1 + 3 * rim]
        h = list(start)
        for q in range(rim):
            pre = bias
            for p in range(taps):
                pre = pre + w[p] * x[q + p]
            dt = recv[slot, span + 1 + rim + q]
            xd = dt * silu(pre)
            for j in range(span):
                h[j] = jnp.exp2(a[j] * dt) * h[j] + btile[j : j + 1, q : q + 1] * xd
        total = recv[slot, span]
        h = [jnp.exp2(a[j] * total) * h[j] + recv[slot, j] for j in range(span)]
        tail = [recv[slot, span + 1 + 2 * rim + q] for q in range(rim)]
        return h, tail

    for q in range(span + rim):
        table[0, q] = zero
    root_end, root_tail = node(0, [zero] * span, [zero] * rim)
    for q, value in enumerate(root_end + root_tail):
        table[1, q] = value
    for k in range(1, FEW + 1):
        end, tail = node(k, root_end, root_tail)
        for q, value in enumerate(end + tail):
            table[1 + k, q] = value

    def reply(k, c):
        to = ((tile + tiles - k // groups) % tiles) * groups + (me + k) % groups
        back[to] = table[sel_ref[to]]

        @pl.when(to != me)
        def _():
            down_out(to).start()

        return c

    lax.fori_loop(0, n, reply, 0)
    own = pltpu.make_async_copy(back.at[me], starts.at[me], local_sem)
    own.start()
    own.wait()

    def full_pass(r, unused):
        b = (tile + r) % tiles
        for g in range(groups):
            source = b * groups + g

            @pl.when(source != me)
            def _():
                down_in(source).wait_recv()

        for q in range(rim):
            xs[pl.ds(PAD - rim + q, 8, stride=rows), :] = starts[b * groups, span + q]
        prepare(rows, b, length, 0, x_ref, dt_ref, w_ref, bias_ref, xs, us, dts, xds)
        a = [a_ref[b, j] for j in range(states)]

        def steps(i, carry):
            h = list(carry)
            for k in range(STEPS):
                t = i * STEPS + k
                dt = tile_of(dts, rows, t)
                xd = tile_of(xds, rows, t)
                parts = []
                for j in range(states):
                    h[j] = jnp.exp2(a[j] * dt) * h[j] + maps_ref[t * 2 * states + j] * xd
                    part = maps_ref[t * 2 * states + states + j] * h[j]
                    if j < 2:
                        parts.append(part)
                    else:
                        parts[j % 2] = parts[j % 2] + part
                ys[pl.ds(t, 8, stride=rows), :] = parts[0] + parts[1]
            return tuple(h)

        start = tuple(starts[b * groups + j // span, j % span] for j in range(states))
        lax.fori_loop(0, slots // STEPS, steps, start)
        t_ids = lax.broadcasted_iota(jnp.int32, (slots, 128), 0)
        live = (t_ids < length).astype(jnp.float32)
        for c in range(8):
            cols = column(b, c)
            rows_c = pl.ds(c * rows, slots)
            y = ys[rows_c, :] + skip_ref[0:1, cols] * us[rows_c, :]
            gate = silu(z_ref[0, :, cols].astype(jnp.float32)) * live
            out_ref[0, :, cols] = (y * gate).astype(jnp.bfloat16)
        return unused

    lax.fori_loop(0, tiles, full_pass, 0)

    def finish(k, c):
        up_out((me + k) % n).wait_send()
        down_out((me + k) % n).wait_send()
        return c

    lax.fori_loop(1, n, finish, 0)


def body(
    conv_input, gate_input, step_size, state_maps, a_log, conv_weight, conv_bias, skip_gain,
    owner_slot, parent, lengths,
):
    n = owner_slot.shape[0]
    _, slots, inner = conv_input.shape
    states = a_log.shape[0]
    taps = conv_weight.shape[0]
    rim = taps - 1
    tiles = inner // TILE
    groups = n // tiles
    span = states // groups
    rows = slots + PAD
    message = span + 2 + 3 * rim

    me = lax.axis_index("req")
    ids = jnp.arange(n, dtype=jnp.int32)
    holds = owner_slot[None, :] == ids[:, None]
    my_len = jnp.sum(jnp.where(owner_slot == me, lengths, 0)).reshape(1)
    source = jnp.where(ids == 0, 0, jnp.where(ids <= FEW, 1, parent + 1))
    sel = jnp.sum(jnp.where(holds, source[None, :], 0), 1)

    maps = state_maps[0].astype(jnp.float32)
    flat_maps = maps.T.reshape(-1)
    btile = jnp.pad(maps[:states].reshape(groups, span, slots), ((0, 0), (0, 8 - span), (0, 0)))
    btile = btile[:, :, :128]
    a2 = (-LOG2E * jnp.exp(a_log)).reshape(states, tiles, 8, 128).transpose(1, 0, 2, 3)
    w_tiles = conv_weight.astype(jnp.float32).reshape(taps, tiles, 8, 128)
    bias_tiles = conv_bias.reshape(tiles, 8, 128)
    bias_row = conv_bias[None]
    skip_row = skip_gain[None]

    smem = pl.BlockSpec(memory_space=pltpu.SMEM)
    vmem = pl.BlockSpec(memory_space=pltpu.VMEM)
    columns = pltpu.VMEM((8 * rows, 128), jnp.float32)

    return pl.pallas_call(
        functools.partial(tree_kernel, groups),
        out_shape=jax.ShapeDtypeStruct((1, slots, inner), jnp.bfloat16),
        in_specs=[smem] * 4 + [vmem] * 10,
        out_specs=vmem,
        scratch_shapes=[columns] * 5
        + [
            pltpu.VMEM((n, message, 8, 128), jnp.float32),
            pltpu.VMEM((n, message, 8, 128), jnp.float32),
            pltpu.VMEM((FEW + 2, span + rim, 8, 128), jnp.float32),
            pltpu.VMEM((n, span + rim, 8, 128), jnp.float32),
            pltpu.VMEM((n, span + rim, 8, 128), jnp.float32),
        ]
        + [pltpu.SemaphoreType.DMA((n,))] * 4
        + [pltpu.SemaphoreType.DMA],
        compiler_params=pltpu.CompilerParams(
            vmem_limit_bytes=VMEM_LIMIT, collective_id=0, has_side_effects=True
        ),
        name="tree_scan",
    )(
        my_len, flat_maps, owner_slot, sel, conv_input, step_size, gate_input, btile, a2,
        conv_weight.astype(jnp.float32), bias_row, skip_row, w_tiles, bias_tiles,
    )


def solution(mesh):
    blocks = P(("parts", "req"), None, None)
    return jax.shard_map(
        body,
        mesh=mesh,
        in_specs=(
            blocks, blocks, blocks, blocks,
            P(), P(), P(), P(),
            P("parts"), P("parts"), P("parts"),
        ),
        out_specs=blocks,
        check_vma=False,
    )
```

time: 110 us -> 86.1 us (0.78)
  the two profiles are of different devices: /device:TPU:21 before, /device:TPU:30 now
where the time goes in v2:
time: 86.1 us; the launch traced here: 85.7 us
  Pallas kernels  75.2 us (87%)
  other arithmetic  5.58 us (6%)
  local copies, waits for them, and re-layouts  4.84 us (6%)
    pallas_call x1, Pallas kernels, body(): pl.pallas_call(functools.partial(tree_kernel, groups), out_shape=jax.Shap...  75.2 us
    unnamed x15, local copies, waits for them, and re-layouts  4.63 us
    unnamed x2, other arithmetic  1.99 us

profile of v2, /device:TPU:30, one launch (start us, length us, event | category | flops | bytes accessed | tf_op | source)
XLA Modules:
  0.0 85.7 jit_solution(2479229014213307436)
XLA Ops:
  0.0 0.0 copy-start.5
  0.0 0.0 copy-start.3
  0.0 0.0 copy-start.4
  0.0 0.0 copy-start
  0.0 1.5 %fusion = s32[]{:T(128)} fusion(s32[16]{0:T(128)} %param.21, s32[16]{0:T(128)} %owner_ref.1, s32[]{:T(128)S(6)} %axis_index.12), kind=kLoop, calls=%fused_computation.11 | loop fusion | flops 47 | bytes 136 | tf_op jit(solution)/shard_map/reduce_sum | solution.py:262
  1.5 0.7 compare_select_fusion.1
  2.1 0.8 select_reduce_fusion.sel_ref
  2.9 0.7 fusion.1
  3.6 0.1 copy.14
  3.7 0.1 reshape.24.maps_ref
  3.8 0.9 %convert_bitcast_fusion = (f32[1,4,64,128]{3,1,2,0:T(4,128)S(1)}, f32[4,8192]{1,0:T(4,128)S(1)}) fusion(bf16[4,8192]{1,0:T(4,128)(2,1)} %param.16), kind=kLoop, calls=%fused_computation.3 | loop fusion | flops 32768 | bytes 327680
  4.7 1.1 %multiply_bitcast_fusion = f32[2,8,64,128]{3,1,2,0:T(8,128)S(1)} fusion(f32[16,8192]{1,0:T(8,128)} %param.15), kind=kLoop, calls=%fused_computation.1 | loop fusion | flops 131072 | bytes 1048576
  5.8 0.1 copy.16
  6.0 0.0 copy-done.5
  6.0 0.0 copy-done.3
  6.0 0.0 copy-done.4
  6.0 0.0 copy-done
  6.0 0.0 copy-start.1
  6.0 1.6 %copy-done.1 = bf16[1,128,8192]{2,1,0:T(8,128)(2,1)S(1)} copy-done((bf16[1,128,8192]{2,1,0:T(8,128)(2,1)S(1)}, bf16[1,128,8192]{2,1,0:T(8,128)(2,1)}, u32[]{:S(2)}) %copy-start.1) | copy-done | bytes 2097176
  7.6 0.0 copy-start.2
  7.6 1.6 %copy-done.2 = bf16[1,128,8192]{2,1,0:T(8,128)(2,1)S(1)} copy-done((bf16[1,128,8192]{2,1,0:T(8,128)(2,1)S(1)}, bf16[1,128,8192]{2,1,0:T(8,128)(2,1)}, u32[]{:S(2)}) %copy-start.2) | copy-done | bytes 2097176
  9.2 75.2 %tree_scan.1 = bf16[1,128,8192]{2,1,0:T(8,128)(2,1)S(1)} custom-call(s32[1]{0:T(128)} %bitcast.len_ref, f32[4096]{0:T(1024)S(1)} %reshape.24.maps_ref, s32[16]{0:T(128)S(1)} %copy-done.5, s32[16]{0:T(128)S(1)} %select_reduce_fusion.sel_ref, bf16[1,128,8192]{2,1,0:T(8,128)(2,1)S(1)} %copy-done, bf16[1,128,8192]{2,1,0:T(8,128)(2,1)S(1)} %copy-done.1, ...), custom_call_target="tpu_custom_call" | custom-call | tf_op jit(solution)/shard_map/tree_scan/pallas_call | solution.py:280
  84.4 1.3 %copy.23 = bf16[1,128,8192]{2,1,0:T(8,128)(2,1)} copy(bf16[1,128,8192]{2,1,0:T(8,128)(2,1)S(1)} %tree_scan.1) | data formatting | bytes 4194304
  (3 shorter events, 0.1 us)
Async XLA Ops:
  0.0 6.0 %copy-start.5 = (s32[16]{0:T(128)S(1)}, s32[16]{0:T(128)}, u32[]{:S(2)}) copy-start(s32[16]{0:T(128)} %owner_ref.1) | copy-start | bytes 196
  0.0 6.0 %copy-start.3 = (f32[8192]{0:T(1024)S(1)}, f32[8192]{0:T(1024)}, u32[]{:S(2)}) copy-start(f32[8192]{0:T(1024)} %param.17) | copy-start | bytes 98308
  0.0 6.0 %copy-start.4 = (f32[8192]{0:T(1024)S(1)}, f32[8192]{0:T(1024)}, u32[]{:S(2)}) copy-start(f32[8192]{0:T(1024)} %param.18) | copy-start | bytes 98308
  0.0 6.0 %copy-start = (bf16[1,128,8192]{2,1,0:T(8,128)(2,1)S(1)}, bf16[1,128,8192]{2,1,0:T(8,128)(2,1)}, u32[]{:S(2)}) copy-start(bf16[1,128,8192]{2,1,0:T(8,128)(2,1)} %x_ref.1) | copy-start | bytes 6291460
  6.0 1.6 %copy-start.1 = (bf16[1,128,8192]{2,1,0:T(8,128)(2,1)S(1)}, bf16[1,128,8192]{2,1,0:T(8,128)(2,1)}, u32[]{:S(2)}) copy-start(bf16[1,128,8192]{2,1,0:T(8,128)(2,1)} %dt_ref.1) | copy-start | bytes 6291460
  7.6 1.6 %copy-start.2 = (bf16[1,128,8192]{2,1,0:T(8,128)(2,1)S(1)}, bf16[1,128,8192]{2,1,0:T(8,128)(2,1)}, u32[]{:S(2)}) copy-start(bf16[1,128,8192]{2,1,0:T(8,128)(2,1)} %z_ref.1) | copy-start | bytes 6291460

commit v3 on v2

v3 whole, which is shorter than its diff:
```python
import functools
import math

import jax
import jax.numpy as jnp
from jax import lax
from jax.experimental import pallas as pl
from jax.experimental.pallas import tpu as pltpu
from jax.sharding import PartitionSpec as P

FEW = 4
TILE = 1024
PAD = 8
STEPS = 16
LOG2E = math.log2(math.e)
VMEM_LIMIT = 40 * 1024 * 1024


def silu(v):
    half = 0.5 * v
    return half + half * jnp.tanh(half)


def column(b, c):
    return pl.ds(pl.multiple_of(b * TILE + c * 128, 128), 128)


def tree_kernel(
    groups, len_ref, owner_ref, above_ref, sel_ref, x_ref, dt_ref, z_ref, tail_ref, maps_ref, a_ref,
    w_ref, bias_ref, skip_ref, w_tiles, bias_tiles, out_ref,
    xs, us, dts, xds, ys, heads, tails, picked, history, msg, recv, table, back, starts,
    send_a, recv_a, send_b, recv_b, send1, recv1, send2, recv2, local_sem,
):
    n = msg.shape[0]
    slots = x_ref.shape[1]
    rows = slots + PAD
    tiles, states = a_ref.shape[:2]
    span = states // groups
    taps = w_ref.shape[0]
    rim = taps - 1
    me = lax.axis_index("req")
    tile = me // groups
    lead = me % groups == 0
    first = (me % groups) * span
    length = len_ref[0]
    zero = jnp.zeros((8, 128), jnp.float32)

    barrier = pltpu.get_barrier_semaphore()

    def greet(k, c):
        pl.semaphore_signal(
            barrier, inc=1, device_id={"req": (me + k) % n}, device_id_type=pl.DeviceIdType.MESH
        )
        return c

    lax.fori_loop(1, n, greet, 0)
    pl.semaphore_wait(barrier, n - 1)

    def copy(src, dst, slot, sends, recvs, sent, device):
        return pltpu.make_async_remote_copy(
            src_ref=src, dst_ref=dst, send_sem=sends.at[sent], recv_sem=recvs.at[slot],
            device_id={"req": device}, device_id_type=pl.DeviceIdType.MESH,
        )

    def own(src, dst):
        mine = pltpu.make_async_copy(src, dst, local_sem)
        mine.start()
        mine.wait()

    def tail_out(b):
        return copy(tail_ref.at[b], tails.at[me], me, send_a, recv_a, b, b * groups)

    def tail_in(source):
        return copy(tail_ref.at[0], tails.at[source], source, send_a, recv_a, 0, source)

    def past_out(to):
        return copy(picked.at[to], history.at[tile], tile, send_b, recv_b, to, to)

    def past_in(b):
        return copy(picked.at[0], history.at[b], b, send_b, recv_b, 0, b * groups)

    def up_out(to):
        return copy(msg.at[to], recv.at[me], me, send1, recv1, to, to)

    def up_in(source):
        return copy(msg.at[source], recv.at[source], source, send1, recv1, source, source)

    def down_out(to):
        return copy(back.at[to], starts.at[me], me, send2, recv2, to, to)

    def down_in(source):
        return copy(back.at[source], starts.at[source], source, send2, recv2, source, source)

    def away(device, action):
        @pl.when(device != me)
        def _():
            action()

    def send_tail(r, c):
        b = (tile + r) % tiles
        away(b * groups, lambda: tail_out(b).start())
        return c

    lax.fori_loop(0, tiles, send_tail, 0)
    for c in range(8):
        xs[pl.ds(c * rows, PAD), :] = zero
    t_ids = lax.broadcasted_iota(jnp.int32, (slots, 128), 0)
    live = (t_ids < length).astype(jnp.float32)

    def column(b, c):
        return pl.ds(pl.multiple_of(b * TILE + c * 128, 128), 128)

    def base(b, c):
        return pl.multiple_of((b * 8 + c) * rows, 8)

    def tile_rows(b, t):
        return pl.ds(b * 8 * rows + t, 8, stride=rows)

    def prepare(b, carry):
        for c in range(8):
            cols = column(b, c)
            to = pl.ds(base(b, c), slots)
            xs[pl.ds(c * rows + PAD, slots), :] = x_ref[0, :, cols].astype(jnp.float32)
            pre = bias_ref[0:1, cols]
            for k in range(taps):
                pre = pre + w_ref[k : k + 1, cols] * xs[
                    pl.ds(c * rows + PAD - rim + k, slots), :
                ]
            u = silu(pre)
            dt = dt_ref[0, :, cols].astype(jnp.float32) * live
            us[to, :] = u
            dts[to, :] = dt
            xds[to, :] = dt * u
        for q in range(rim):
            heads[b, q] = xs[pl.ds(PAD + q, 8, stride=rows), :]
        return carry

    lax.fori_loop(0, tiles // 2, prepare, 0)

    @pl.when(lead)
    def _():
        own(tail_ref.at[tile], tails.at[me])
        lax.fori_loop(1, n, lambda k, c: (tail_in((me + k) % n).wait_recv(), c)[1], 0)

        def pick(k, c):
            to = ((tile + tiles - k // groups) % tiles) * groups + k % groups
            known = (sel_ref[to] > 0).astype(jnp.float32)
            for q in range(rim):
                picked[to, q] = tails[above_ref[to], q] * known
            away(to, lambda: past_out(to).start())
            return c

        lax.fori_loop(0, n, pick, 0)
        own(picked.at[me], history.at[tile])

    lax.fori_loop(tiles // 2, tiles, prepare, 0)

    def correct(b, carry):
        away(b * groups, lambda: past_in(b).wait_recv())
        x = [history[b, q] for q in range(rim)] + [heads[b, q] for q in range(rim)]
        for q in range(rim):
            pre = bias_tiles[b]
            for k in range(taps):
                pre = pre + w_tiles[k, b] * x[q + k]
            u = silu(pre)
            us[tile_rows(b, q), :] = u
            xds[tile_rows(b, q), :] = dts[tile_rows(b, q), :] * u
        return carry

    lax.fori_loop(0, tiles, correct, 0)

    def state_pass(r, unused):
        b = (tile + r) % tiles
        a = [a_ref[b, j] for j in range(states)]

        def steps(i, carry):
            h, total = list(carry[:-1]), carry[-1]
            for k in range(STEPS):
                t = i * STEPS + k
                dt = dts[tile_rows(b, t), :]
                xd = xds[tile_rows(b, t), :]
                for j in range(states):
                    into = maps_ref[pl.ds(t * 2 * states + j, 1), :]
                    h[j] = jnp.exp2(a[j] * dt) * h[j] + into * xd
                total = total + dt
            return (*h, total)

        out = lax.fori_loop(0, slots // STEPS, steps, (zero,) * (states + 1))
        for g in range(groups):
            to = b * groups + g
            for j in range(span):
                msg[to, j] = out[g * span + j]
            msg[to, span] = out[states]
            away(to, lambda: up_out(to).start())
        return unused

    lax.fori_loop(0, tiles, state_pass, 0)
    own(msg.at[me], recv.at[me])
    lax.fori_loop(1, n, lambda k, c: (up_in((me + k) % n).wait_recv(), c)[1], 0)

    for j in range(span):
        a = a_ref[tile, first + j]
        root = recv[owner_ref[0], j]
        table[0, j] = zero
        table[1, j] = root
        for k in range(1, FEW + 1):
            slot = owner_ref[k]
            table[1 + k, j] = jnp.exp2(a * recv[slot, span]) * root + recv[slot, j]

    def reply(k, c):
        to = ((tile + tiles - k // groups) % tiles) * groups + (me + k) % groups
        back[to] = table[sel_ref[to]]
        away(to, lambda: down_out(to).start())
        return c

    lax.fori_loop(0, n, reply, 0)
    own(back.at[me], starts.at[me])

    def full_pass(r, unused):
        b = (tile + r) % tiles
        for g in range(groups):
            source = b * groups + g
            away(source, lambda: down_in(source).wait_recv())
        a = [a_ref[b, j] for j in range(states)]

        def steps(i, carry):
            h = list(carry)
            for k in range(STEPS):
                t = i * STEPS + k
                dt = dts[tile_rows(b, t), :]
                xd = xds[tile_rows(b, t), :]
                parts = []
                for j in range(states):
                    into = maps_ref[pl.ds(t * 2 * states + j, 1), :]
                    h[j] = jnp.exp2(a[j] * dt) * h[j] + into * xd
                    part = maps_ref[pl.ds(t * 2 * states + states + j, 1), :] * h[j]
                    if j < 2:
                        parts.append(part)
                    else:
                        parts[j % 2] = parts[j % 2] + part
                ys[pl.ds(t, 8, stride=rows), :] = parts[0] + parts[1]
            return tuple(h)

        start = tuple(starts[b * groups + j // span, j % span] for j in range(states))
        lax.fori_loop(0, slots // STEPS, steps, start)
        for c in range(8):
            cols = column(b, c)
            y = ys[pl.ds(c * rows, slots), :] + skip_ref[0:1, cols] * us[pl.ds(base(b, c), slots), :]
            gate = silu(z_ref[0, :, cols].astype(jnp.float32)) * live
            out_ref[0, :, cols] = (y * gate).astype(jnp.bfloat16)
        return unused

    lax.fori_loop(0, tiles, full_pass, 0)

    def finish(k, c):
        to = (me + k) % n
        up_out(to).wait_send()
        down_out(to).wait_send()

        @pl.when(lead)
        def _():
            past_out(to).wait_send()

        return c

    lax.fori_loop(1, n, finish, 0)
    lax.fori_loop(
        0, tiles, lambda b, c: (away(b * groups, lambda: tail_out(b).wait_send()), c)[1], 0
    )


def body(
    conv_input, gate_input, step_size, state_maps, a_log, conv_weight, conv_bias, skip_gain,
    owner_slot, parent, lengths,
):
    n = owner_slot.shape[0]
    _, slots, inner = conv_input.shape
    states = a_log.shape[0]
    taps = conv_weight.shape[0]
    rim = taps - 1
    tiles = inner // TILE
    groups = n // tiles
    span = states // groups
    rows = slots + PAD

    me = lax.axis_index("req")
    ids = jnp.arange(n, dtype=jnp.int32)
    holds = owner_slot[None, :] == ids[:, None]
    my_len = jnp.sum(jnp.where(owner_slot == me, lengths, 0))
    source = jnp.where(ids == 0, 0, jnp.where(ids <= FEW, 1, parent + 1))
    sel = jnp.sum(jnp.where(holds, source[None, :], 0), 1)
    above = jnp.sum(jnp.where(ids[None, :] == jnp.maximum(sel - 1, 0)[:, None], owner_slot, 0), 1)

    maps = jnp.broadcast_to(
        state_maps[0].astype(jnp.float32).T.reshape(-1, 1), (slots * 2 * states, 128)
    )
    tail = lax.dynamic_slice_in_dim(conv_input[0], my_len - rim, rim, 0).astype(jnp.float32)
    tail = tail.reshape(rim, tiles, 8, 128).transpose(1, 0, 2, 3)
    a2 = (-LOG2E * jnp.exp(a_log)).reshape(states, tiles, 8, 128).transpose(1, 0, 2, 3)
    weight = conv_weight.astype(jnp.float32)
    w_tiles = weight.reshape(taps, tiles, 8, 128)
    bias_tiles = conv_bias.reshape(tiles, 8, 128)

    smem = pl.BlockSpec(memory_space=pltpu.SMEM)
    vmem = pl.BlockSpec(memory_space=pltpu.VMEM)
    one = pltpu.VMEM((8 * rows, 128), jnp.float32)
    every = pltpu.VMEM((tiles * 8 * rows, 128), jnp.float32)

    def boxes(*lead):
        return pltpu.VMEM((*lead, 8, 128), jnp.float32)

    return pl.pallas_call(
        functools.partial(tree_kernel, groups),
        out_shape=jax.ShapeDtypeStruct((1, slots, inner), jnp.bfloat16),
        in_specs=[smem] * 4 + [vmem] * 11,
        out_specs=vmem,
        scratch_shapes=[one, every, every, every, one]
        + [boxes(tiles, rim), boxes(n, rim), boxes(n, rim), boxes(tiles, rim)]
        + [boxes(n, span + 1), boxes(n, span + 1), boxes(FEW + 2, span)]
        + [boxes(n, span), boxes(n, span)]
        + [pltpu.SemaphoreType.DMA((count,)) for count in (tiles, n, n, tiles, n, n, n, n)]
        + [pltpu.SemaphoreType.DMA],
        compiler_params=pltpu.CompilerParams(
            vmem_limit_bytes=VMEM_LIMIT, collective_id=0, has_side_effects=True
        ),
        name="tree_scan",
    )(
        my_len.reshape(1), owner_slot, above, sel, conv_input, step_size, gate_input, tail, maps,
        a2, weight, conv_bias[None], skip_gain[None], w_tiles, bias_tiles,
    )


def solution(mesh):
    blocks = P(("parts", "req"), None, None)
    return jax.shard_map(
        body,
        mesh=mesh,
        in_specs=(
            blocks, blocks, blocks, blocks,
            P(), P(), P(), P(),
            P("parts"), P("parts"), P("parts"),
        ),
        out_specs=blocks,
        check_vma=False,
    )
```

time: 86.1 us -> 70.7 us (0.82)
  the two profiles are of different devices: /device:TPU:30 before, /device:TPU:0 now
where the time goes in v3:
time: 70.7 us; the launch traced here: 70.4 us
  Pallas kernels  57.8 us (82%)
  other arithmetic  7.4 us (10%)
  local copies, waits for them, and re-layouts  3.69 us (5%)
  between operations  1.44 us (2%)
    pallas_call x1, Pallas kernels, body(): pl.pallas_call(functools.partial(tree_kernel, groups), out_shape=jax.Shap...  57.8 us
    unnamed x3, other arithmetic  3.12 us
    unnamed x15, local copies, waits for them, and re-layouts  2.87 us

profile of v3, /device:TPU:0, one launch (start us, length us, event | category | flops | bytes accessed | tf_op | source)
XLA Modules:
  0.0 70.4 jit_solution(12538874089253136643)
XLA Ops:
  0.0 1.3 %fusion = s32[]{:T(128)} fusion(s32[16]{0:T(128)} %param.21, s32[16]{0:T(128)} %owner_ref.1, s32[]{:T(128)S(6)} %axis_index.12), kind=kLoop, calls=%fused_computation.15 | loop fusion | flops 47 | bytes 136 | tf_op jit(solution)/shard_map/reduce_sum | solution.py:289
  2.6 0.7 compare_select_fusion.1
  3.3 0.8 %select_reduce_fusion.1.sel_ref = s32[16]{0:T(128)S(1)} fusion(s32[16]{0:T(128)S(1)} %compare_select_fusion.1, s32[16]{0:T(128)} %owner_ref.1), kind=kLoop, calls=%fused_computation.9 | loop fusion | flops 752 | bytes 192 | tf_op jit(solution)/shard_map/reduce_sum | solution.py:291
  4.0 0.8 %select_reduce_fusion.above_ref = s32[16]{0:T(128)S(1)} fusion(s32[16]{0:T(128)S(1)} %add_maximum_fusion, s32[16]{0:T(128)} %owner_ref.1), kind=kLoop, calls=%fused_computation.8 | loop fusion | flops 752 | bytes 192 | tf_op jit(solution)/shard_map/reduce_sum | solution.py:292
  4.9 0.7 convert_bitcast_fusion.2
  5.6 0.1 copy.16
  5.7 0.0 copy-start.2
  5.7 0.1 reshape.31
  5.8 1.1 %convert_bitcast_fusion = f32[1,3,64,128]{3,1,2,0:T(4,128)S(1)} fusion(bf16[1,128,8192]{2,1,0:T(8,128)(2,1)} %x_ref.1, s32[]{:T(128)S(6)} %select_n.27), kind=kLoop, calls=%fused_computation.3 | loop fusion | flops 24576 | bytes 147460
  6.9 0.9 %convert_bitcast_fusion.1 = (f32[1,4,64,128]{3,1,2,0:T(4,128)S(1)}, f32[4,8192]{1,0:T(4,128)S(1)}) fusion(bf16[4,8192]{1,0:T(4,128)(2,1)} %param.16), kind=kLoop, calls=%fused_computation.6 | loop fusion | flops 32768 | bytes 327680
  7.8 0.0 copy-start.3
  7.8 0.0 copy-start.4
  7.8 1.1 %multiply_bitcast_fusion = f32[2,8,64,128]{3,1,2,0:T(8,128)S(1)} fusion(f32[16,8192]{1,0:T(8,128)} %param.15), kind=kLoop, calls=%fused_computation.1 | loop fusion | flops 131072 | bytes 1048576
  9.0 0.0 copy-start
  9.0 0.0 copy-start.1
  9.0 0.0 copy-start.5
  9.0 0.1 copy.19
  9.2 0.6 broadcast_in_dim.52.maps_ref
  9.8 0.0 copy-done.2
  9.8 0.0 copy-done.3
  9.8 0.0 copy-done.4
  9.8 0.8 %copy-done = bf16[1,128,8192]{2,1,0:T(8,128)(2,1)S(1)} copy-done((bf16[1,128,8192]{2,1,0:T(8,128)(2,1)S(1)}, bf16[1,128,8192]{2,1,0:T(8,128)(2,1)}, u32[]{:S(2)}) %copy-start) | copy-done | bytes 2097176
  10.6 0.6 copy-done.1
  11.2 0.0 copy-done.5
  11.2 57.8 %tree_scan.1 = bf16[1,128,8192]{2,1,0:T(8,128)(2,1)S(1)} custom-call(s32[1]{0:T(128)} %bitcast.len_ref, s32[16]{0:T(128)S(1)} %copy-done.5, s32[16]{0:T(128)S(1)} %select_reduce_fusion.above_ref, s32[16]{0:T(128)S(1)} %select_reduce_fusion.1.sel_ref, bf16[1,128,8192]{2,1,0:T(8,128)(2,1)S(1)} %copy-done, bf16[1,128,8192]{2,1,0:T(8,128)(2,1)S(1)} %copy-done.1, ...), custom_call_target="tpu_custom_call" | custom-call | tf_op jit(solution)/shard_map/tree_scan/pallas_call | solution.py:312
  69.0 1.3 %copy.29 = bf16[1,128,8192]{2,1,0:T(8,128)(2,1)} copy(bf16[1,128,8192]{2,1,0:T(8,128)(2,1)S(1)} %tree_scan.1) | data formatting | bytes 4194304
  (4 shorter events, 0.1 us)
Async XLA Ops:
  5.7 4.1 %copy-start.2 = (bf16[1,128,8192]{2,1,0:T(8,128)(2,1)S(1)}, bf16[1,128,8192]{2,1,0:T(8,128)(2,1)}, u32[]{:S(2)}) copy-start(bf16[1,128,8192]{2,1,0:T(8,128)(2,1)} %z_ref.1) | copy-start | bytes 6291460
  7.8 2.0 %copy-start.3 = (f32[8192]{0:T(1024)S(1)}, f32[8192]{0:T(1024)}, u32[]{:S(2)}) copy-start(f32[8192]{0:T(1024)} %param.17) | copy-start | bytes 98308
  7.8 2.0 %copy-start.4 = (f32[8192]{0:T(1024)S(1)}, f32[8192]{0:T(1024)}, u32[]{:S(2)}) copy-start(f32[8192]{0:T(1024)} %param.18) | copy-start | bytes 98308
  9.0 1.6 %copy-start = (bf16[1,128,8192]{2,1,0:T(8,128)(2,1)S(1)}, bf16[1,128,8192]{2,1,0:T(8,128)(2,1)}, u32[]{:S(2)}) copy-start(bf16[1,128,8192]{2,1,0:T(8,128)(2,1)} %x_ref.1) | copy-start | bytes 6291460
  9.0 2.2 %copy-start.1 = (bf16[1,128,8192]{2,1,0:T(8,128)(2,1)S(1)}, bf16[1,128,8192]{2,1,0:T(8,128)(2,1)}, u32[]{:S(2)}) copy-start(bf16[1,128,8192]{2,1,0:T(8,128)(2,1)} %dt_ref.1) | copy-start | bytes 6291460
  9.0 2.2 %copy-start.5 = (s32[16]{0:T(128)S(1)}, s32[16]{0:T(128)}, u32[]{:S(2)}) copy-start(s32[16]{0:T(128)} %owner_ref.1) | copy-start | bytes 196

commit v4 on v3

--- a/solution.py
+++ b/solution.py
@@ -25,10 +25,28 @@
     return pl.ds(pl.multiple_of(b * TILE + c * 128, 128), 128)
 
 
+def relate_kernel(len_ref, owner_ref, parent_ref, mine_ref, above_ref, sel_ref):
+    n = owner_ref.shape[0]
+    me = lax.axis_index("req")
+    length = 0
+    for k in range(n):
+        length = length + jnp.where(owner_ref[k] == me, len_ref[k], 0)
+    mine_ref[0] = length
+
+    def relate(k, c):
+        kind = jnp.where(k == 0, 0, jnp.where(k <= FEW, 1, parent_ref[k] + 1))
+        to = owner_ref[k]
+        sel_ref[to] = kind
+        above_ref[to] = owner_ref[jnp.maximum(kind - 1, 0)]
+        return c
+
+    lax.fori_loop(0, n, relate, 0)
+
+
 def tree_kernel(
-    groups, len_ref, owner_ref, above_ref, sel_ref, x_ref, dt_ref, z_ref, tail_ref, maps_ref, a_ref,
-    w_ref, bias_ref, skip_ref, w_tiles, bias_tiles, out_ref,
-    xs, us, dts, xds, ys, heads, tails, picked, history, msg, recv, table, back, starts,
+    groups, len_ref, owner_ref, above_ref, sel_ref, x_ref, dt_ref, z_ref, tail_ref, maps_ref, alog_ref,
+    w_ref, bias_ref, skip_ref, out_ref,
+    xs, us, dts, xds, gates, ys, acols, a_ref, w_tiles, heads, tails, picked, history, msg, recv, table, back, starts,
     send_a, recv_a, send_b, recv_b, send1, recv1, send2, recv2, local_sem,
 ):
     n = msg.shape[0]
@@ -96,19 +114,19 @@
         def _():
             action()
 
-    def send_tail(r, c):
+    def column(b, c):
+        return pl.ds(pl.multiple_of(b * TILE + c * 128, 128), 128)
+
+    def send_tail(r, cc):
         b = (tile + r) % tiles
         away(b * groups, lambda: tail_out(b).start())
-        return c
+        return cc
 
     lax.fori_loop(0, tiles, send_tail, 0)
     for c in range(8):
         xs[pl.ds(c * rows, PAD), :] = zero
     t_ids = lax.broadcasted_iota(jnp.int32, (slots, 128), 0)
     live = (t_ids < length).astype(jnp.float32)
-
-    def column(b, c):
-        return pl.ds(pl.multiple_of(b * TILE + c * 128, 128), 128)
 
     def base(b, c):
         return pl.multiple_of((b * 8 + c) * rows, 8)
@@ -131,6 +149,12 @@
             us[to, :] = u
             dts[to, :] = dt
             xds[to, :] = dt * u
+            acols[pl.ds(c * 24, states), :] = -LOG2E * jnp.exp(alog_ref[:, cols])
+            for k in range(taps):
+                w_tiles[b, k, c : c + 1, :] = w_ref[k : k + 1, cols]
+            w_tiles[b, taps, c : c + 1, :] = bias_ref[0:1, cols]
+        for j in range(states):
+            a_ref[b, j] = acols[pl.ds(j, 8, stride=24), :]
         for q in range(rim):
             heads[b, q] = xs[pl.ds(PAD + q, 8, stride=rows), :]
         return carry
@@ -159,9 +183,9 @@
         away(b * groups, lambda: past_in(b).wait_recv())
         x = [history[b, q] for q in range(rim)] + [heads[b, q] for q in range(rim)]
         for q in range(rim):
-            pre = bias_tiles[b]
+            pre = w_tiles[b, taps]
             for k in range(taps):
-                pre = pre + w_tiles[k, b] * x[q + k]
+                pre = pre + w_tiles[b, k] * x[q + k]
             u = silu(pre)
             us[tile_rows(b, q), :] = u
             xds[tile_rows(b, q), :] = dts[tile_rows(b, q), :] * u
@@ -195,6 +219,17 @@
         return unused
 
     lax.fori_loop(0, tiles, state_pass, 0)
+
+    def gate(b, carry):
+        for c in range(8):
+            cols = column(b, c)
+            at = pl.ds(base(b, c), slots)
+            value = silu(z_ref[0, :, cols].astype(jnp.float32)) * live
+            gates[at, :] = value
+            us[at, :] = skip_ref[0:1, cols] * us[at, :] * value
+        return carry
+
+    lax.fori_loop(0, tiles, gate, 0)
     own(msg.at[me], recv.at[me])
     lax.fori_loop(1, n, lambda k, c: (up_in((me + k) % n).wait_recv(), c)[1], 0)
 
@@ -245,9 +280,9 @@
         lax.fori_loop(0, slots // STEPS, steps, start)
         for c in range(8):
             cols = column(b, c)
-            y = ys[pl.ds(c * rows, slots), :] + skip_ref[0:1, cols] * us[pl.ds(base(b, c), slots), :]
-            gate = silu(z_ref[0, :, cols].astype(jnp.float32)) * live
-            out_ref[0, :, cols] = (y * gate).astype(jnp.bfloat16)
+            at = pl.ds(base(b, c), slots)
+            y = ys[pl.ds(c * rows, slots), :] * gates[at, :] + us[at, :]
+            out_ref[0, :, cols] = y.astype(jnp.bfloat16)
         return unused
 
     lax.fori_loop(0, tiles, full_pass, 0)
@@ -283,26 +318,20 @@
     span = states // groups
     rows = slots + PAD
 
-    me = lax.axis_index("req")
-    ids = jnp.arange(n, dtype=jnp.int32)
-    holds = owner_slot[None, :] == ids[:, None]
-    my_len = jnp.sum(jnp.where(owner_slot == me, lengths, 0))
-    source = jnp.where(ids == 0, 0, jnp.where(ids <= FEW, 1, parent + 1))
-    sel = jnp.sum(jnp.where(holds, source[None, :], 0), 1)
-    above = jnp.sum(jnp.where(ids[None, :] == jnp.maximum(sel - 1, 0)[:, None], owner_slot, 0), 1)
-
     maps = jnp.broadcast_to(
         state_maps[0].astype(jnp.float32).T.reshape(-1, 1), (slots * 2 * states, 128)
     )
-    tail = lax.dynamic_slice_in_dim(conv_input[0], my_len - rim, rim, 0).astype(jnp.float32)
-    tail = tail.reshape(rim, tiles, 8, 128).transpose(1, 0, 2, 3)
-    a2 = (-LOG2E * jnp.exp(a_log)).reshape(states, tiles, 8, 128).transpose(1, 0, 2, 3)
-    weight = conv_weight.astype(jnp.float32)
-    w_tiles = weight.reshape(taps, tiles, 8, 128)
-    bias_tiles = conv_bias.reshape(tiles, 8, 128)
-
     smem = pl.BlockSpec(memory_space=pltpu.SMEM)
     vmem = pl.BlockSpec(memory_space=pltpu.VMEM)
+    my_len, above, sel = pl.pallas_call(
+        relate_kernel,
+        out_shape=[jax.ShapeDtypeStruct((count,), jnp.int32) for count in (1, n, n)],
+        in_specs=[smem] * 3,
+        out_specs=[smem] * 3,
+        name="relate",
+    )(lengths, owner_slot, parent)
+    tail = lax.dynamic_slice_in_dim(conv_input[0], my_len[0] - rim, rim, 0).astype(jnp.float32)
+    tail = tail.reshape(rim, tiles, 8, 128).transpose(1, 0, 2, 3)
     one = pltpu.VMEM((8 * rows, 128), jnp.float32)
     every = pltpu.VMEM((tiles * 8 * rows, 128), jnp.float32)
 
@@ -312,9 +341,11 @@
     return pl.pallas_call(
         functools.partial(tree_kernel, groups),
         out_shape=jax.ShapeDtypeStruct((1, slots, inner), jnp.bfloat16),
-        in_specs=[smem] * 4 + [vmem] * 11,
+        in_specs=[smem] * 4 + [vmem] * 9,
         out_specs=vmem,
-        scratch_shapes=[one, every, every, every, one]
+        scratch_shapes=[one, every, every, every, every, one]
+        + [pltpu.VMEM((8 * 24, 128), jnp.float32)]
+        + [boxes(tiles, states), boxes(tiles, taps + 1)]
         + [boxes(tiles, rim), boxes(n, rim), boxes(n, rim), boxes(tiles, rim)]
         + [boxes(n, span + 1), boxes(n, span + 1), boxes(FEW + 2, span)]
         + [boxes(n, span), boxes(n, span)]
@@ -325,8 +356,8 @@
         ),
         name="tree_scan",
     )(
-        my_len.reshape(1), owner_slot, above, sel, conv_input, step_size, gate_input, tail, maps,
-        a2, weight, conv_bias[None], skip_gain[None], w_tiles, bias_tiles,
+        my_len, owner_slot, above, sel, conv_input, step_size, gate_input, tail, maps,
+        a_log, conv_weight.astype(jnp.float32), conv_bias[None], skip_gain[None],
     )
 
 

time: 70.7 us -> 68.5 us (0.969)
  other arithmetic: 7.4 us -> 2.56 us
  local copies, waits for them, and re-layouts: 3.69 us -> 5.31 us
  Pallas kernels: 57.8 us -> 58.9 us
    reduce_sum x3 -> x0, other arithmetic: 2.92 us -> none  [the longest x1 1.31 us: body(): my_len = jnp.sum(jnp.where(owner_slot == me, lengths, 0))]
    unnamed x3 -> x1, other arithmetic: 3.12 us -> 1 us
    unnamed x15 -> x19, local copies, waits for them, and re-layouts: 2.87 us -> 4.53 us
    pallas_call x0 -> x1, Pallas kernels: none -> 1.54 us  [body(): pl.pallas_call(relate_kernel, out_shape=[jax.ShapeDtypeStruct((count,), j...]
    convert_element_type x0 -> x1, other arithmetic: none -> 0.86 us  [body(): conv_weight.astype(jnp.float32)]
where the time goes in v4:
time: 68.5 us; the launch traced here: 68.2 us
  Pallas kernels  58.9 us (86%)
  local copies, waits for them, and re-layouts  5.31 us (8%)
  other arithmetic  2.56 us (4%)
  between operations  1.42 us (2%)
    pallas_call x1, Pallas kernels, body(): pl.pallas_call(functools.partial(tree_kernel, groups), out_shape=jax.Shap...  57.3 us
    unnamed x19, local copies, waits for them, and re-layouts  4.53 us
    pallas_call x1, Pallas kernels, body(): pl.pallas_call(relate_kernel, out_shape=[jax.ShapeDtypeStruct((count,), j...  1.54 us

profile of v4, /device:TPU:0, one launch (start us, length us, event | category | flops | bytes accessed | tf_op | source)
XLA Modules:
  0.0 68.2 jit_solution(16510616720886559439)
XLA Ops:
  0.0 0.0 copy-start.6
  0.0 0.0 copy-start
  0.0 0.0 copy-start.5
  0.0 0.0 copy-start.4
  0.0 0.0 copy-start.3
  0.0 1.5 %relate.1 = (s32[1]{0:T(128)}, s32[16]{0:T(128)}, s32[16]{0:T(128)}) custom-call(s32[16]{0:T(128)} %len_ref.1, s32[16]{0:T(128)} %owner_ref.3, s32[16]{0:T(128)} %parent_ref.1), custom_call_target="tpu_custom_call" | custom-call | tf_op jit(solution)/shard_map/relate/pallas_call | solution.py:326
  1.6 0.0 copy-start.7
  1.6 0.0 copy-start.8
  2.9 0.7 %convert_bitcast_fusion.1 = f32[128,32]{0,1:T(8,128)S(1)} fusion(bf16[1,32,128]{2,1,0:T(8,128)(2,1)} %param.14), kind=kLoop, calls=%fused_computation.3 | loop fusion | flops 4096 | bytes 24576 | tf_op jit(solution)/shard_map/broadcast_in_dim | solution.py:321
  3.6 0.1 copy.13
  3.7 0.1 reshape.13
  3.8 1.0 %convert_bitcast_fusion = f32[1,3,64,128]{3,1,2,0:T(4,128)S(1)} fusion(bf16[1,128,8192]{2,1,0:T(8,128)(2,1)} %x_ref.1, s32[]{:T(128)S(6)} %select_n.3), kind=kLoop, calls=%fused_computation | loop fusion | flops 24576 | bytes 147460
  4.8 0.9 %convert_element_type.14.w_ref = f32[4,8192]{1,0:T(4,128)S(1)} convert(bf16[4,8192]{1,0:T(4,128)(2,1)} %param.16) | non-fusion elementwise | flops 32768 | bytes 196608 | tf_op jit(solution)/shard_map/convert_element_type | solution.py:360
  5.6 0.6 broadcast_in_dim.18.maps_ref
  6.2 0.0 copy-done.6
  6.3 0.0 copy-done
  6.3 0.0 copy-done.5
  6.3 0.0 copy-done.4
  6.3 0.0 copy-done.3
  6.3 0.0 copy-done.7
  6.3 0.0 copy-done.8
  6.3 0.0 copy-start.1
  6.3 1.6 %copy-done.1 = bf16[1,128,8192]{2,1,0:T(8,128)(2,1)S(1)} copy-done((bf16[1,128,8192]{2,1,0:T(8,128)(2,1)S(1)}, bf16[1,128,8192]{2,1,0:T(8,128)(2,1)}, u32[]{:S(2)}) %copy-start.1) | copy-done | bytes 2097176
  7.9 0.0 copy-start.2
  7.9 1.6 %copy-done.2 = bf16[1,128,8192]{2,1,0:T(8,128)(2,1)S(1)} copy-done((bf16[1,128,8192]{2,1,0:T(8,128)(2,1)S(1)}, bf16[1,128,8192]{2,1,0:T(8,128)(2,1)}, u32[]{:S(2)}) %copy-start.2) | copy-done | bytes 2097176
  9.5 57.3 %tree_scan.1 = bf16[1,128,8192]{2,1,0:T(8,128)(2,1)S(1)} custom-call(s32[1]{0:T(128)} %get-tuple-element.8.len_ref, s32[16]{0:T(128)S(1)} %copy-done.6, s32[16]{0:T(128)S(1)} %copy-done.7, s32[16]{0:T(128)S(1)} %copy-done.8, bf16[1,128,8192]{2,1,0:T(8,128)(2,1)S(1)} %copy-done, bf16[1,128,8192]{2,1,0:T(8,128)(2,1)S(1)} %copy-done.1, ...), custom_call_target="tpu_custom_call" | custom-call | tf_op jit(solution)/shard_map/tree_scan/pallas_call | solution.py:341
  66.8 1.3 %copy.19 = bf16[1,128,8192]{2,1,0:T(8,128)(2,1)} copy(bf16[1,128,8192]{2,1,0:T(8,128)(2,1)S(1)} %tree_scan.1) | data formatting | bytes 4194304
  (1 shorter events, 0.0 us)
Async XLA Ops:
  0.0 6.2 %copy-start.6 = (s32[16]{0:T(128)S(1)}, s32[16]{0:T(128)}, u32[]{:S(2)}) copy-start(s32[16]{0:T(128)} %owner_ref.3) | copy-start | bytes 196
  0.0 6.3 %copy-start = (bf16[1,128,8192]{2,1,0:T(8,128)(2,1)S(1)}, bf16[1,128,8192]{2,1,0:T(8,128)(2,1)}, u32[]{:S(2)}) copy-start(bf16[1,128,8192]{2,1,0:T(8,128)(2,1)} %x_ref.1) | copy-start | bytes 6291460
  0.0 6.3 %copy-start.5 = (f32[8192]{0:T(1024)S(1)}, f32[8192]{0:T(1024)}, u32[]{:S(2)}) copy-start(f32[8192]{0:T(1024)} %param.18) | copy-start | bytes 98308
  0.0 6.3 %copy-start.4 = (f32[8192]{0:T(1024)S(1)}, f32[8192]{0:T(1024)}, u32[]{:S(2)}) copy-start(f32[8192]{0:T(1024)} %param.17) | copy-start | bytes 98308
  0.0 6.3 %copy-start.3 = (f32[16,8192]{1,0:T(8,128)S(1)}, f32[16,8192]{1,0:T(8,128)}, u32[]{:S(2)}) copy-start(f32[16,8192]{1,0:T(8,128)} %alog_ref.1) | copy-start | bytes 1572868
  1.6 4.7 %copy-start.7 = (s32[16]{0:T(128)S(1)}, s32[16]{0:T(128)}, u32[]{:S(2)}) copy-start(s32[16]{0:T(128)} %get-tuple-element.9.above_ref) | copy-start | bytes 196
  1.6 4.7 %copy-start.8 = (s32[16]{0:T(128)S(1)}, s32[16]{0:T(128)}, u32[]{:S(2)}) copy-start(s32[16]{0:T(128)} %get-tuple-element.10.sel_ref) | copy-start | bytes 196
  6.3 1.6 %copy-start.1 = (bf16[1,128,8192]{2,1,0:T(8,128)(2,1)S(1)}, bf16[1,128,8192]{2,1,0:T(8,128)(2,1)}, u32[]{:S(2)}) copy-start(bf16[1,128,8192]{2,1,0:T(8,128)(2,1)} %dt_ref.1) | copy-start | bytes 6291460
  7.9 1.6 %copy-start.2 = (bf16[1,128,8192]{2,1,0:T(8,128)(2,1)S(1)}, bf16[1,128,8192]{2,1,0:T(8,128)(2,1)}, u32[]{:S(2)}) copy-start(bf16[1,128,8192]{2,1,0:T(8,128)(2,1)} %z_ref.1) | copy-start | bytes 6291460
